TPU v7x, 32 devices: a whole 2x2x4 slice. The times are simulated.
32 devices in a mesh: lat: 8 (over y, x, core), lon: 4 (over z).
Axes of the slice: x: 2, y: 2, z: 4, core: 2. Of those that a mesh axis runs over, the one named last changes fastest.
Arguments:
- height: float32 [2048, 8640], P('lat', 'lon'), may hold values from -6 to 8
- east_vel: float32 [2048, 8640], P('lat', 'lon'), may hold values from -3 to 3
- north_vel: float32 [2048, 8640], P('lat', 'lon'), may hold values from -3 to 3
- sea_depth: float32 [2048, 8640], P('lat', 'lon'), may hold values from 1 to 4
- sea_mask: int32 [2048, 8640], P('lat', 'lon'), may hold values 0 or 1
- forcing: bfloat16 [2, 8, 2048, 8640], P(None, None, 'lat', 'lon'), may hold values from -6 to 6
- thickness: float32 [8], replicated, may hold values from 1 to 10
- cycle_length: int32 [2048], P('lat'), may hold values from 180 to 720
- slot_order: int32 [720], replicated, may hold values from 0 to 719, each once
- love_index: int32 [720], replicated, may hold values from 0 to 63
- love_table: float32 [64], replicated, may hold values from 0.5 to 1.5
Outputs:
- height_out: float32 [2048, 8640], P('lat', 'lon')
- east_out: float32 [2048, 8640], P('lat', 'lon')
- north_out: float32 [2048, 8640], P('lat', 'lon')
- load_coeffs: float32 [2, 720, 720], P(None, 'lon', 'lat')
- sal_field: float32 [2048, 8640], P('lat', 'lon')
Inputs may be any that keep to these rules, and one draw needn't show every extreme that they name: `slot_order`: every order appears once.
All inputs are finite; a program needn't handle non-finite values. No bound on the sum of `sea_mask` on one device may be relied on, other than what follows from the above.
Results may differ from a plain program's by a relative error of at most 0.014.
Values may be sent and summed in bfloat16 or wider, within the bound.
No kernel may reach another device: no remote copies, remote signals or barrier semaphores. Data moves between devices by JAX's collectives and lax.ppermute only.
A program may use at most 192 MiB of HBM per device.

v0:
```python
import math
import jax
import jax.numpy as jnp
from jax import lax
from jax.sharding import PartitionSpec as P

NLON = 8640
LMAX = 720
LEVELS = 8
ITERS = 10
LOVE_ROWS = 64
time_step = 0.6
drag_coeff = 0.5
tide_speed = 0.1
coriolis_scale = 0.8
degree_block = 24
rescale_limit = 1e20
rescale_log = 20.0 * math.log(10.0)


def padded(block, sides, width, periodic):
    for axis, dim in sides:
        count = lax.axis_size(axis)
        forward = [(i, i + 1) for i in range(count - 1)]
        if periodic:
            forward.append((count - 1, 0))
        backward = [(target, source) for source, target in forward]
        low = lax.ppermute(
            lax.slice_in_dim(block, block.shape[dim] - width, None, axis=dim), axis, forward
        )
        high = lax.ppermute(lax.slice_in_dim(block, 0, width, axis=dim), axis, backward)
        block = jnp.concatenate([low, block, high], axis=dim)
    return block


def cycle_geometry(row_ids, cycle_count):
    latitude = (row_ids.astype(jnp.float32) + 0.5) * (math.pi / cycle_count) - 0.5 * math.pi
    return (jnp.sin(latitude), jnp.cos(latitude))


def start_logs():
    counter = jnp.arange(LMAX).astype(jnp.float32)
    log_terms = jnp.where(
        counter > 0.0, 0.5 * jnp.log((2.0 * counter + 1.0) / jnp.maximum(2.0 * counter, 1.0)), 0.0
    )
    return jnp.cumsum(log_terms)


def next_row(degree, order_col, sine_row, prev_one, prev_two, scale_log):
    deg_gap = degree * degree - order_col * order_col
    past_one = degree >= order_col + 1.0
    past_two = degree >= order_col + 2.0
    lead_sq = jnp.where(
        past_one, (4.0 * degree * degree - 1.0) / jnp.where(past_one, deg_gap, 1.0), 0.0
    )
    lag_num = (2.0 * degree + 1.0) * ((degree - 1.0) * (degree - 1.0) - order_col * order_col)
    lag_sq = jnp.where(
        past_two, lag_num / jnp.where(past_two, (2.0 * degree - 3.0) * deg_gap, 1.0), 0.0
    )
    value_row = jnp.where(
        degree == order_col,
        1.0,
        jnp.sqrt(lead_sq) * sine_row * prev_one - jnp.sqrt(lag_sq) * prev_two,
    )
    large = jnp.abs(value_row) > rescale_limit
    factor = jnp.where(large, 1.0 / rescale_limit, 1.0)
    value_row = value_row * factor
    carried = prev_one * factor
    scale_log = scale_log + jnp.where(large, rescale_log, 0.0)
    output = value_row * jnp.exp(scale_log)
    return (value_row, carried, scale_log, output)


def wave_table(orders, part_ids, lon_ids):
    phases = (orders[:, None] * lon_ids[None, :] % NLON).astype(jnp.float32) * (
        2.0 * math.pi / NLON
    )
    return jnp.where(part_ids[:, None] == 0, jnp.cos(phases), -jnp.sin(phases))


def forward_entries(orders, part_ids, lon_ids):
    return (wave_table(orders, part_ids, lon_ids) / NLON).astype(jnp.bfloat16)


def inverse_entries(orders, part_ids, lon_ids):
    weight_gain = jnp.where(orders == 0, 1.0, 2.0)
    return (weight_gain[:, None] * wave_table(orders, part_ids, lon_ids)).astype(jnp.bfloat16)


def slot_orders(column_ids, per_owner, slot_order):
    owner_ids = column_ids // (2 * per_owner)
    part_ids = column_ids // per_owner % 2
    flat_ids = owner_ids * per_owner + column_ids % per_owner
    matches = flat_ids[:, None] == jnp.arange(LMAX, dtype=jnp.int32)[None, :]
    orders = jnp.sum(jnp.where(matches, slot_order[None, :], 0), axis=1)
    return (orders, part_ids)


def legendre_loop(orders_f, log_m, sines, cosines):
    order_col = orders_f[:, None]
    start_scale = log_m[:, None] + order_col * jnp.log(cosines)[None, :]
    sine_row = sines[None, :]
    empty = jnp.zeros(start_scale.shape, jnp.float32)
    tables = jnp.zeros((orders_f.shape[0], LMAX, sines.shape[0]), jnp.bfloat16)

    def fill_block(block_id, loop_state):
        prev_one, prev_two, scale_log, filled = loop_state
        new_rows = []
        for within in range(degree_block):
            degree = (block_id * degree_block + within).astype(jnp.float32)
            value_row, carried, scale_log, output = next_row(
                degree, order_col, sine_row, prev_one, prev_two, scale_log
            )
            prev_two = carried
            prev_one = value_row
            new_rows.append(output.astype(jnp.bfloat16))
        stacked = jnp.stack(new_rows, axis=1)
        filled = lax.dynamic_update_slice(
            filled,
            stacked,
            (jnp.int32(0), (block_id * degree_block).astype(jnp.int32), jnp.int32(0)),
        )
        return (prev_one, prev_two, scale_log, filled)

    result = lax.fori_loop(0, LMAX // degree_block, fill_block, (empty, empty, start_scale, tables))
    return result[3]


def local(
    height,
    east_vel,
    north_vel,
    sea_depth,
    sea_mask,
    forcing,
    thickness,
    cycle_length,
    slot_order,
    love_index,
    love_table,
):
    lat_rows, lon_cols = height.shape
    lat_parts = lax.axis_size("lat")
    lon_parts = lax.axis_size("lon")
    cycle_count = lat_rows * lat_parts
    per_owner = LMAX // lon_parts
    first_row = lax.axis_index("lat") * lat_rows
    first_col = lax.axis_index("lon") * lon_cols
    row_ids = first_row + jnp.arange(lat_rows, dtype=jnp.int32)
    sines, cosines = cycle_geometry(row_ids, cycle_count)
    inside = (row_ids > 0) & (row_ids < cycle_count - 1)
    wet_cells = jnp.where(inside[:, None] & (sea_mask > 0), 1.0, 0.0).astype(jnp.float32)
    level_weights = thickness / jnp.sum(thickness)
    east_push = jnp.zeros(height.shape, jnp.float32)
    north_push = jnp.zeros(height.shape, jnp.float32)
    for level in range(LEVELS):
        east_push = east_push + level_weights[level] * forcing[0, level].astype(jnp.float32)
        north_push = north_push + level_weights[level] * forcing[1, level].astype(jnp.float32)
    margin = 2 * ITERS
    stacked = jnp.stack([height, east_vel, north_vel, sea_depth, wet_cells, east_push, north_push])
    widened = padded(stacked.astype(jnp.bfloat16), (("lat", 1),), margin, False).astype(
        stacked.dtype
    )
    widened = padded(widened.astype(jnp.bfloat16), (("lon", 2),), margin, True).astype(
        widened.dtype
    )
    wide_rows = first_row - margin + jnp.arange(lat_rows + 2 * margin, dtype=jnp.int32)
    wide_sines, wide_cosines = cycle_geometry(wide_rows, cycle_count)
    coriolis = coriolis_scale * wide_sines[:, None]
    height, east, north = (widened[0], widened[1], widened[2])
    depth_wide, wet_wide, push_east, push_north = (widened[3], widened[4], widened[5], widened[6])
    for substep in range(ITERS):
        east_flux = depth_wide * east
        north_flux = depth_wide * north
        height = height[1:-1, 1:-1] - time_step * wet_wide[1:-1, 1:-1] * (
            0.5
            * (
                east_flux[1:-1, 2:]
                - east_flux[1:-1, :-2]
                + (north_flux[2:, 1:-1] - north_flux[:-2, 1:-1])
            )
        )
        east_slope = 0.5 * (height[1:-1, 2:] - height[1:-1, :-2])
        north_slope = 0.5 * (height[2:, 1:-1] - height[:-2, 1:-1])
        height = height[1:-1, 1:-1]
        east = east[2:-2, 2:-2]
        north = north[2:-2, 2:-2]
        depth_wide = depth_wide[2:-2, 2:-2]
        wet_wide = wet_wide[2:-2, 2:-2]
        push_east = push_east[2:-2, 2:-2]
        push_north = push_north[2:-2, 2:-2]
        coriolis = coriolis[2:-2]
        flow_speed = jnp.sqrt(east * east + north * north + tide_speed * tide_speed)
        damping = 1.0 + time_step * drag_coeff * flow_speed / jnp.where(
            wet_wide > 0.0, depth_wide, 1.0
        )
        east_new = (
            wet_wide * (east + time_step * (coriolis * north - east_slope + push_east)) / damping
        )
        north = (
            wet_wide * (north + time_step * (-coriolis * east - north_slope + push_north)) / damping
        )
        east = east_new
    surface_load = (wet_cells * height).astype(jnp.bfloat16)
    own_lon = first_col + jnp.arange(lon_cols, dtype=jnp.int32)
    column_ids = jnp.arange(2 * per_owner * lax.axis_size("lon"), dtype=jnp.int32)
    orders, part_ids = slot_orders(column_ids, per_owner, slot_order)
    entries = forward_entries(orders, part_ids, own_lon)
    spectra = lax.psum_scatter(
        lax.dot_general(
            entries, surface_load, (((1,), (1,)), ((), ())), preferred_element_type=jnp.float32
        ).astype(jnp.bfloat16),
        "lon",
        scatter_dimension=0,
        tiled=True,
    ).astype(jnp.float32)
    spectra = spectra.reshape(2, per_owner, lat_rows)
    own_orders = lax.dynamic_slice(slot_order, (lax.axis_index("lon") * per_owner,), (per_owner,))
    retained = own_orders[:, None] < cycle_length[None, :]
    weight_lat = 0.5 * cosines * (math.pi / cycle_count)
    weighted = jnp.where(retained[None], spectra * weight_lat[None, None, :], 0.0).astype(
        jnp.bfloat16
    )
    log_starts = start_logs()
    own_logs = jnp.sum(
        jnp.where(
            own_orders[:, None] == jnp.arange(LMAX, dtype=jnp.int32)[None, :],
            log_starts[None, :],
            0.0,
        ),
        axis=1,
    )
    tables = legendre_loop(own_orders.astype(jnp.float32), own_logs, sines, cosines)
    sums = jnp.einsum("knj,pkj->pkn", tables, weighted, preferred_element_type=jnp.float32)
    load_factor = jnp.sum(
        jnp.where(
            love_index[:, None] == jnp.arange(LOVE_ROWS, dtype=jnp.int32)[None, :],
            love_table[None, :],
            0.0,
        ),
        axis=1,
    )
    share_width = LMAX // lat_parts
    report_scale = math.sqrt(NLON * cycle_count)
    sums = lax.psum(sums, "lat")
    coefficients = sums * load_factor[None, None, :]
    scaled = coefficients.astype(jnp.bfloat16)
    own_coeffs = lax.dynamic_slice_in_dim(
        coefficients, lax.axis_index("lat") * share_width, share_width, 2
    )
    load_coeffs = report_scale * own_coeffs
    synthesis = jnp.einsum(
        "knj,pkn->pkj", tables, scaled, preferred_element_type=jnp.float32
    ).astype(jnp.bfloat16)
    synthesis = synthesis.reshape(2 * per_owner, lat_rows)
    shard_rows = lax.all_gather(synthesis, "lon", axis=0, tiled=True)
    column_ids = jnp.arange(shard_rows.shape[0], dtype=jnp.int32)
    orders, part_ids = slot_orders(column_ids, per_owner, slot_order)
    entries = inverse_entries(orders, part_ids, own_lon)
    sal_field = lax.dot_general(
        shard_rows, entries, (((0,), (0,)), ((), ())), preferred_element_type=jnp.float32
    )
    return (height, east, north, load_coeffs, sal_field)


def solution(mesh):
    in_specs = (
        P("lat", "lon"),
        P("lat", "lon"),
        P("lat", "lon"),
        P("lat", "lon"),
        P("lat", "lon"),
        P(None, None, "lat", "lon"),
        P(),
        P("lat"),
        P(),
        P(),
        P(),
    )
    out_specs = (
        P("lat", "lon"),
        P("lat", "lon"),
        P("lat", "lon"),
        P(None, "lon", "lat"),
        P("lat", "lon"),
    )
    return jax.shard_map(local, mesh=mesh, in_specs=in_specs, out_specs=out_specs, check_vma=False)
```

profile of v0, /device:TPU:0, one launch (start us, length us, event | category | flops | bytes accessed | tf_op | source)
XLA Modules:
  0.0 1059.0 jit_solution(18119053795163229721)
XLA Ops:
  94.9 56.4 %concatenate.7 = bf16[7,296,2200]{1,2,0:T(8,128)(2,1)} concatenate(bf16[7,296,20]{1,2,0:T(8,128)(2,1)S(1)} %collective-permute-done.2, bf16[7,296,2160]{1,2,0:T(8,128)(2,1)} %copy-done.7, bf16[7,296,20]{1,2,0:T(8,128)(2,1)S(1)} %collective-permute-done.3), dimensions={2} | concatenate | bytes 18233600 | tf_op jit(solution)/shard_map/concatenate | solution.py:32
  151.3 13.3 %convert_element_type.790 = f32[7,296,2200]{1,2,0:T(8,128)} convert(bf16[7,296,2200]{1,2,0:T(8,128)(2,1)} %concatenate.7) | non-fusion elementwise | flops 4558400 | bytes 27350400 | tf_op jit(solution)/shard_map/convert_element_type | solution.py:164
  171.9 14.8 %slice_bitcast_fusion.1 = (f32[296,2200]{0,1:T(8,128)S(1)}, f32[296,2200]{0,1:T(8,128)}, f32[296,2200]{0,1:T(8,128)}, f32[296,2200]{0,1:T(8,128)}, f32[296,2200]...) fusion(f32[7,296,2200]{1,2,0:T(8,128)} %convert_element_type.790), kind=kLoop, calls=%fused_computation.498 | loop fusion | bytes 36467200 | tf_op jit(solution)/shard_map/squeeze | solution.py:171
  196.4 13.0 %slice_multiply_fusion.11 = (f32[292,2196]{0,1:T(8,128)S(1)}, f32[292,2196]{0,1:T(8,128)}, f32[292,2196]{0,1:T(8,128)}, f32[292,2196]{0,1:T(8,128)}) fusion(f32[296,2200]{0,1:T(8,128)S(1)} %copy-done.3, f32[296,2200]{0,1:T(8,128)S(1)} %get-tuple-element.672, f32[294,2198]{0,1:T(8,128)S(1)} %fusion.173, f32[296,2200]{0,1:T(8,128)} %get-tuple-element.674, ...), kind=kLoop, calls=%fused_computation.711 | loop fusion | flops 18595728 | bytes 35911328 | tf_op jit(solution)/shard_map/mul | solution.py:173
  218.2 19.6 %slice_multiply_fusion.15 = (f32[288,2192]{0,1:T(8,128)}, f32[288,2192]{0,1:T(8,128)}, f32[288,2192]{0,1:T(8,128)}, f32[288,2192]{0,1:T(8,128)}) fusion(f32[296,2200]{0,1:T(8,128)} %get-tuple-element.676, f32[296,2200]{0,1:T(8,128)S(1)} %get-tuple-element.672, f32[290,2194]{0,1:T(8,128)} %fusion.157, f32[292,2196]{0,1:T(8,128)} %get-tuple-element.684, ...), kind=kLoop, calls=%fused_computation.715 | loop fusion | flops 18307584 | bytes 35354880 | tf_op jit(solution)/shard_map/mul | solution.py:173
  248.8 19.3 %slice_multiply_fusion.13 = (f32[284,2188]{0,1:T(8,128)}, f32[284,2188]{0,1:T(8,128)}, f32[284,2188]{0,1:T(8,128)}, f32[284,2188]{0,1:T(8,128)}) fusion(f32[296,2200]{0,1:T(8,128)} %get-tuple-element.676, f32[296,2200]{0,1:T(8,128)S(1)} %get-tuple-element.672, f32[286,2190]{0,1:T(8,128)} %fusion.193, f32[288,2192]{0,1:T(8,128)} %get-tuple-element.682, ...), kind=kLoop, calls=%fused_computation.713 | loop fusion | flops 18020368 | bytes 34800224 | tf_op jit(solution)/shard_map/mul | solution.py:173
  278.1 12.9 %slice_multiply_fusion.19 = (f32[280,2184]{0,1:T(8,128)}, f32[280,2184]{0,1:T(8,128)}, f32[280,2184]{0,1:T(8,128)}, f32[280,2184]{0,1:T(8,128)}) fusion(f32[296,2200]{0,1:T(8,128)S(1)} %copy-done.4, f32[296,2200]{0,1:T(8,128)S(1)} %get-tuple-element.672, f32[282,2186]{0,1:T(8,128)S(1)} %fusion.177, f32[284,2188]{0,1:T(8,128)} %get-tuple-element.688, ...), kind=kLoop, calls=%fused_computation.719 | loop fusion | flops 17734080 | bytes 34247360 | tf_op jit(solution)/shard_map/mul | solution.py:173
  301.2 12.7 %slice_multiply_fusion.17 = (f32[276,2180]{0,1:T(8,128)S(1)}, f32[276,2180]{0,1:T(8,128)}, f32[276,2180]{0,1:T(8,128)}, f32[276,2180]{0,1:T(8,128)}) fusion(f32[296,2200]{0,1:T(8,128)S(1)} %copy-done.4, f32[296,2200]{0,1:T(8,128)S(1)} %get-tuple-element.672, f32[278,2182]{0,1:T(8,128)S(1)} %fusion.225, f32[280,2184]{0,1:T(8,128)} %get-tuple-element.686, ...), kind=kLoop, calls=%fused_computation.717 | loop fusion | flops 17448720 | bytes 33696288 | tf_op jit(solution)/shard_map/mul | solution.py:173
  322.7 19.2 %slice_multiply_fusion.23 = (f32[272,2176]{0,1:T(8,128)}, f32[272,2176]{0,1:T(8,128)}, f32[272,2176]{0,1:T(8,128)}, f32[272,2176]{0,1:T(8,128)}) fusion(f32[296,2200]{0,1:T(8,128)} %get-tuple-element.676, f32[296,2200]{0,1:T(8,128)S(1)} %get-tuple-element.672, f32[274,2178]{0,1:T(8,128)} %fusion.209, f32[276,2180]{0,1:T(8,128)} %get-tuple-element.692, ...), kind=kLoop, calls=%fused_computation.723 | loop fusion | flops 17164288 | bytes 33147008 | tf_op jit(solution)/shard_map/mul | solution.py:173
  341.9 11.0 %fusion.257 = f32[270,2174]{0,1:T(8,128)} fusion(f32[272,2176]{0,1:T(8,128)} %get-tuple-element.689, f32[272,2176]{0,1:T(8,128)} %get-tuple-element.526, f32[296,2200]{0,1:T(8,128)S(1)} %get-tuple-element.677, f32[274,2178]{0,1:T(8,128)} %fusion.209), kind=kLoop, calls=%fused_computation.639 | loop fusion | flops 4108860 | bytes 16435440 | tf_op jit(solution)/shard_map/sub | solution.py:175
  352.9 19.3 %slice_multiply_fusion.21 = (f32[268,2172]{0,1:T(8,128)}, f32[268,2172]{0,1:T(8,128)}, f32[268,2172]{0,1:T(8,128)}, f32[268,2172]{0,1:T(8,128)}) fusion(f32[296,2200]{0,1:T(8,128)} %get-tuple-element.676, f32[296,2200]{0,1:T(8,128)S(1)} %get-tuple-element.672, f32[270,2174]{0,1:T(8,128)} %fusion.257, f32[272,2176]{0,1:T(8,128)} %get-tuple-element.690, ...), kind=kLoop, calls=%fused_computation.721 | loop fusion | flops 16880784 | bytes 32599520 | tf_op jit(solution)/shard_map/mul | solution.py:173
  372.2 11.1 %fusion.241 = f32[266,2170]{0,1:T(8,128)} fusion(f32[268,2172]{0,1:T(8,128)} %get-tuple-element.695, f32[268,2172]{0,1:T(8,128)} %get-tuple-element.522, f32[296,2200]{0,1:T(8,128)S(1)} %get-tuple-element.677, f32[270,2174]{0,1:T(8,128)} %fusion.257), kind=kLoop, calls=%fused_computation.616 | loop fusion | flops 4040540 | bytes 16162160 | tf_op jit(solution)/shard_map/sub | solution.py:175
  383.4 18.4 %slice_multiply_fusion.27 = (f32[264,2168]{0,1:T(8,128)}, f32[264,2168]{0,1:T(8,128)}, f32[264,2168]{0,1:T(8,128)}, f32[264,2168]{0,1:T(8,128)}) fusion(f32[296,2200]{0,1:T(8,128)} %get-tuple-element.676, f32[296,2200]{0,1:T(8,128)S(1)} %get-tuple-element.672, f32[266,2170]{0,1:T(8,128)} %fusion.241, f32[268,2172]{0,1:T(8,128)} %get-tuple-element.696, ...), kind=kLoop, calls=%fused_computation.727 | loop fusion | flops 16598208 | bytes 32053824 | tf_op jit(solution)/shard_map/mul | solution.py:173
  401.7 11.3 %fusion.289 = f32[262,2166]{0,1:T(8,128)} fusion(f32[264,2168]{0,1:T(8,128)} %get-tuple-element.693, f32[264,2168]{0,1:T(8,128)} %get-tuple-element.518, f32[296,2200]{0,1:T(8,128)S(1)} %get-tuple-element.677, f32[266,2170]{0,1:T(8,128)} %fusion.241), kind=kLoop, calls=%fused_computation.687 | loop fusion | flops 3972444 | bytes 15889776 | tf_op jit(solution)/shard_map/sub | solution.py:175
  413.1 19.2 %slice_multiply_fusion.25 = (f32[260,2164]{0,1:T(8,128)}, f32[260,2164]{0,1:T(8,128)}, f32[260,2164]{0,1:T(8,128)}, f32[260,2164]{0,1:T(8,128)}) fusion(f32[296,2200]{0,1:T(8,128)} %get-tuple-element.676, f32[296,2200]{0,1:T(8,128)S(1)} %get-tuple-element.672, f32[262,2166]{0,1:T(8,128)} %fusion.289, f32[264,2168]{0,1:T(8,128)} %get-tuple-element.694, ...), kind=kLoop, calls=%fused_computation.725 | loop fusion | flops 16316560 | bytes 31509920 | tf_op jit(solution)/shard_map/mul | solution.py:173
  443.4 14.7 %fusion.307 = (f32[256,2160]{0,1:T(8,128)}, f32[256,2160]{0,1:T(8,128)}, f32[256,2160]{0,1:T(8,128)S(1)}) fusion(f32[296,2200]{0,1:T(8,128)S(1)} %copy-done.2, f32[258,2162]{0,1:T(8,128)} %fusion.273, f32[296,2200]{0,1:T(8,128)} %get-tuple-element.676, f32[260,2164]{0,1:T(8,128)} %get-tuple-element.700, f32[260,2164]{0,1:T(8,128)} %get-tuple-element.515, ...), kind=kLoop, calls=%fused_computation.734 | loop fusion | flops 14929920 | bytes 30967808 | tf_op jit(solution)/shard_map/div | solution.py:201
  458.9 55.8 %fusion.302 = bf16[1440,256]{1,0:T(8,128)(2,1)} fusion(s32[2160]{0:T(1024)S(1)} %copy-done.23, s32[1440]{0:T(1024)S(1)} %copy-done.20, pred[1440]{0:T(1024)(128)(4,1)S(1)} %copy-done.36, bf16[256,2160]{0,1:T(8,128)(2,1)S(1)} %fusion.394), kind=kOutput, calls=%fused_computation.728 | convolution fusion | flops 1633328640 | bytes 1859040 | tf_op jit(solution)/shard_map/dot_general | solution.py:210
  514.7 21.1 %broadcast_in_dim.923.clone = bf16[180,720,256]{2,1,0:T(8,128)(2,1)} broadcast(bf16[]{:T(256)} %constant.625.clone.1), dimensions={} | broadcast | bytes 66355200 | tf_op jit(solution)/shard_map/broadcast_in_dim | solution.py:104
  535.9 330.9 %while.23 = (s32[]{:T(128)}, f32[180,256]{1,0:T(8,128)S(1)}, f32[180,256]{1,0:T(8,128)S(1)}, f32[180,256]{1,0:T(8,128)S(1)}, bf16[180,720,256]{2,1,0:T(8,128)(2,...) while((s32[]{:T(128)}, f32[180,256]{1,0:T(8,128)S(1)}, ...), condition=%wide.region_7.8_spmd.clone, body=%wide.region_6.7_spmd.clone.sunk | while | flops 42912776 | bytes 26192132 | solution.py:125
  868.0 26.2 %convolution_bitcast_fusion = f32[2,180,720]{2,0,1:T(2,128)} fusion(bf16[180,720,256]{2,1,0:T(8,128)(2,1)} %get-tuple-element.332, f32[2,180,256]{2,1,0:T(8,128)S(1)} %reshape.2027, pred[180,256]{1,0:T(8,128)(4,1)S(1)} %broadcast_compare_fusion, f32[256]{0:T(256)S(1)} %broadcast_multiply_fusion.1), kind=kOutput, calls=%fused_computation.752 | convolution fusion | flops 132986880 | bytes 67807744 | tf_op jit(solution)/shard_map/knj,pkj->pkn/dot_general | solution.py:234
  894.4 56.9 %all-reduce.3.cloned.1.call-done = f32[2,180,720]{2,0,1:T(2,128)} async-done(((f32[2,180,720]{2,0,1:T(2,128)}), f32[2,180,720]{2,0,1:T(2,128)}) %all-reduce.3.cloned.1.call-update) | async-done | bytes 1036816 | tf_op jit(solution)/shard_map/psum | solution.py:245
  952.9 23.5 %fusion.318 = bf16[2,180,256]{2,0,1:T(2,128)(2,1)S(1)} fusion(bf16[180,720,256]{2,1,0:T(8,128)(2,1)} %get-tuple-element.332, f32[2,180,720]{2,0,1:T(2,128)S(1)} %broadcast_multiply_fusion), kind=kOutput, calls=%fused_computation.754 | convolution fusion | flops 133061760 | bytes 67576320 | tf_op jit(solution)/shard_map/knj,pkn->pkj/dot_general | solution.py:252
  977.4 18.6 %all_gather.3 = bf16[1440,256]{1,0:T(8,128)(2,1)S(1)} all-gather(bf16[360,256]{1,0:T(8,128)(2,1)S(1)} %reshape.2023), channel_id=1, replica_groups=mesh['lat'=8,'lon'=4] {'lon'}, dimensions={0}, use_global_device_ids=true | all-gather | bytes 921600 | tf_op jit(solution)/shard_map/all_gather | solution.py:256
  996.0 55.8 %fusion.150 = f32[256,2160]{0,1:T(8,128)} fusion(bf16[1440,256]{1,0:T(8,128)(2,1)S(1)} %all_gather.3, f32[1440]{0:T(1024)S(1)} %compare_select_fusion, s32[2160]{0:T(1024)S(1)} %copy-done.23, s32[1440]{0:T(1024)S(1)} %copy-done.20, pred[1440]{0:T(1024)(128)(4,1)S(1)} %copy-done.36), kind=kOutput, calls=%fused_computation.472 | convolution fusion | flops 1632960000 | bytes 2970720 | tf_op jit(solution)/shard_map/dot_general | solution.py:260
  (1506 shorter events, 491.3 us)
Async XLA Ops:
  7.2 859.8 %reduce-scatter.2.cloned.1.call-start = ((), (), s32[]{:S(2)}) async-start(), calls=%async_computation.1 | async-start | bytes 921600 | tf_op jit(solution)/shard_map/reduce_scatter | solution.py:209
  12.5 14.3 %copy-start.10 = (bf16[2,8,256,2160]{2,3,1,0:T(8,128)(2,1)S(1)}, bf16[2,8,256,2160]{2,3,1,0:T(8,128)(2,1)}, u32[]{:S(2)}) copy-start(bf16[2,8,256,2160]{2,3,1,0:T(8,128)(2,1)} %param.18) | copy-start | bytes 53084164
  43.2 12.4 %copy-start.32 = (s32[720]{0:T(1024)S(1)}, s32[720]{0:T(1024)}, u32[]{:S(2)}) copy-start(s32[720]{0:T(1024)} %param.21) | copy-start | bytes 8644
  43.2 20.2 %collective-permute-start.1 = (bf16[7,20,2160]{2,0,1:T(8,128)(2,1)S(1)}, bf16[7,20,2160]{2,0,1:T(8,128)(2,1)S(1)}, u32[]{:S(2)}, u32[]{:S(2)}) collective-permute-start(bf16[7,20,2160]{2,0,1:T(8,128)(2,1)S(1)} %copy.76), channel_id=1, source_target_pairs={{4,0},{8,4},{12,8},{16,12},{20,16},{24,20},{28,24},{5,1},{9,5},{13... | collective-permute-start | bytes 1814408 | tf_op jit(solution)/shard_map/ppermute | solution.py:31
  48.6 11.4 %collective-permute-start = (bf16[7,20,2160]{2,0,1:T(8,128)(2,1)S(1)}, bf16[7,20,2160]{2,0,1:T(8,128)(2,1)S(1)}, u32[]{:S(2)}, u32[]{:S(2)}) collective-permute-start(bf16[7,20,2160]{2,0,1:T(8,128)(2,1)S(1)} %copy.75), channel_id=1, source_target_pairs={{0,4},{4,8},{8,12},{12,16},{16,20},{20,24},{24,28},{1,5},{5,9},{9,... | collective-permute-start | bytes 1814408 | tf_op jit(solution)/shard_map/ppermute | solution.py:28
  81.7 8.9 collective-permute-start.3
  86.8 8.1 collective-permute-start.2
  341.9 11.0 %copy-start.28 = (f32[268]{0:T(512)S(1)}, f32[268]{0:T(512)}, u32[]{:S(2)}) copy-start(f32[268]{0:T(512)} %get-tuple-element.444) | copy-start | bytes 3220
  372.2 11.1 %copy-start.26 = (f32[264]{0:T(512)S(1)}, f32[264]{0:T(512)}, u32[]{:S(2)}) copy-start(f32[264]{0:T(512)} %get-tuple-element.442) | copy-start | bytes 3172
  372.2 11.1 %copy-start.27 = (f32[264]{0:T(512)S(1)}, f32[264]{0:T(512)}, u32[]{:S(2)}) copy-start(f32[264]{0:T(512)} %get-tuple-element.443) | copy-start | bytes 3172
  401.7 11.3 %copy-start.24 = (f32[260]{0:T(512)S(1)}, f32[260]{0:T(512)}, u32[]{:S(2)}) copy-start(f32[260]{0:T(512)} %get-tuple-element.440) | copy-start | bytes 3124
  401.7 11.3 %copy-start.25 = (f32[260]{0:T(512)S(1)}, f32[260]{0:T(512)}, u32[]{:S(2)}) copy-start(f32[260]{0:T(512)} %get-tuple-element.441) | copy-start | bytes 3124
  443.3 14.8 %copy-start.12 = (pred[256,2160]{0,1:T(8,128)(4,1)S(1)}, pred[256,2160]{0,1:T(8,128)(4,1)}, u32[]{:S(2)}) copy-start(pred[256,2160]{0,1:T(8,128)(4,1)} %get-tuple-element.551) | copy-start | bytes 1658884
  458.1 56.5 %copy-start.11 = (f32[256,2160]{0,1:T(8,128)}, f32[256,2160]{0,1:T(8,128)S(1)}, u32[]{:S(2)}) copy-start(f32[256,2160]{0,1:T(8,128)S(1)} %get-tuple-element.705) | copy-start | bytes 6635524
  514.6 436.6 %all-reduce.3.cloned.1.call-start = ((), (), s32[]{:S(2)}) async-start(), calls=%async_computation.2 | async-start | bytes 2211840 | tf_op jit(solution)/shard_map/psum | solution.py:245
  514.7 21.2 %copy-start.5 = (f32[180,256]{1,0:T(8,128)S(1)}, f32[180,256]{1,0:T(8,128)}, u32[]{:S(2)}) copy-start(f32[180,256]{1,0:T(8,128)} %custom-call.1) | copy-start | bytes 552964
  514.7 21.2 %copy-start.6 = (f32[180,256]{1,0:T(8,128)S(1)}, f32[180,256]{1,0:T(8,128)}, u32[]{:S(2)}) copy-start(f32[180,256]{1,0:T(8,128)} %custom-call) | copy-start | bytes 552964
  514.7 21.2 %copy-start.9 = (f32[180,256]{1,0:T(8,128)S(1)}, f32[180,256]{1,0:T(8,128)}, u32[]{:S(2)}) copy-start(f32[180,256]{1,0:T(8,128)} %multiply_add_fusion) | copy-start | bytes 552964
  514.7 21.2 %copy-start.17 = (f32[180]{0:T(256)S(1)}, f32[180]{0:T(256)}, u32[]{:S(2)}) copy-start(f32[180]{0:T(256)} %get-tuple-element.512) | copy-start | bytes 2164
  514.7 21.2 %copy-start.19 = (f32[180]{0:T(256)S(1)}, f32[180]{0:T(256)}, u32[]{:S(2)}) copy-start(f32[180]{0:T(256)} %copy-done.18) | copy-start | bytes 2164
  535.9 330.9 %copy-start.22 = (s32[180]{0:T(256)S(1)}, s32[180]{0:T(256)}, u32[]{:S(2)}) copy-start(s32[180]{0:T(256)} %copy-done.21) | copy-start | bytes 2164
  535.9 330.9 %copy-start.37 = (s32[256]{0:T(256)S(1)}, s32[256]{0:T(256)}, u32[]{:S(2)}) copy-start(s32[256]{0:T(256)} %param.20) | copy-start | bytes 3076
  867.9 26.3 %copy-start.35 = (s32[720]{0:T(1024)S(1)}, s32[720]{0:T(1024)}, u32[]{:S(2)}) copy-start(s32[720]{0:T(1024)} %param.22) | copy-start | bytes 8644
  867.9 26.3 %copy-start.38 = (f32[64]{0:T(128)S(1)}, f32[64]{0:T(128)}, u32[]{:S(2)}) copy-start(f32[64]{0:T(128)} %param.23) | copy-start | bytes 772
  (21 other events, 136.3 us)
Sparse Core Ops, SparseCore 0:
  514.8 22.8 reduce-scatter.1
  894.3 56.8 all-reduce.2
where the time goes:
time: 1070 us; the launch traced here: 1060 us
  other arithmetic  604 us (56%)
  local copies, waits for them, and re-layouts  178 us (17%)
  matrix products  161 us (15%)
  waiting for transfers between devices  64.3 us (6%)
  blocking collectives  18.6 us (2%)
  between operations  15.1 us (1%)
    while x690, other arithmetic  226 us
    mul x10, other arithmetic, local(): east_flux = depth_wide * east  161 us
    sub x10, other arithmetic, local(): height[1:-1, 1:-1]  103 us
    psum x1, waiting for transfers between devices, local(): sums = lax.psum(sums, 'lat')  56.9 us
    dynamic_update_slice x30, local copies, waits for them, and re-layouts, fill_block(): lax.dynamic_update_slice(filled, stacked, (jnp.int32(0), (block_id * degr...  56.7 us
    concatenate x1, local copies, waits for them, and re-layouts, padded(): block = jnp.concatenate([low, block, high], axis=dim)  56.4 us
    dot_general x1, matrix products, local(): lax.dot_general(shard_rows, entries, (((0,), (0,)), ((), ())), preferred_...  55.8 us
    dot_general x1, matrix products, local(): lax.dot_general(entries, surface_load, (((1,), (1,)), ((), ())), preferre...  55.8 us
  transfers between devices with their start and end apart: 6, of which 3 were waited for; matrix products, arithmetic and copies ran while one was open for 34% of the time, Pallas kernels for 0%

commit v1 on v0

--- a/solution.py
+++ b/solution.py
@@ -242,7 +242,9 @@
     )
     share_width = LMAX // lat_parts
     report_scale = math.sqrt(NLON * cycle_count)
-    sums = lax.psum(sums, "lat")
+    sums = sums
+    for hop in (1, 2, 4):
+        sums = sums + lax.ppermute(sums, "lat", [(dev, dev ^ hop) for dev in range(8)])
     coefficients = sums * load_factor[None, None, :]
     scaled = coefficients.astype(jnp.bfloat16)
     own_coeffs = lax.dynamic_slice_in_dim(

time: 1070 us -> 1070 us (level)
    psum x1 -> x0, waiting for transfers between devices: 56.9 us -> none  [local(): sums = lax.psum(sums, 'lat')]
    ppermute x0 -> x3, waiting for transfers between devices: none -> 51.2 us  [local(): lax.ppermute(sums, 'lat', [(dev, dev ^ hop) for dev in range(8)])]
  transfers between devices with their start and end apart: 6 -> 8, of which waited for: 3 -> 5; matrix products, arithmetic and copies ran while one was open for 34% -> 34% of each run, Pallas kernels for 0% -> 0%
where the time goes in v1:
time: 1070 us; the launch traced here: 1060 us
  other arithmetic  604 us (56%)
  local copies, waits for them, and re-layouts  178 us (17%)
  matrix products  160 us (15%)
  waiting for transfers between devices  58.5 us (5%)
  blocking collectives  17.1 us (2%)
  starting transfers between devices  15.3 us (1%)
  between operations  15.1 us (1%)
    while x690, other arithmetic  226 us
    mul x10, other arithmetic, local(): east_flux = depth_wide * east  161 us
    sub x10, other arithmetic, local(): height[1:-1, 1:-1]  103 us
    dynamic_update_slice x30, local copies, waits for them, and re-layouts, fill_block(): lax.dynamic_update_slice(filled, stacked, (jnp.int32(0), (block_id * degr...  56.7 us
    concatenate x1, local copies, waits for them, and re-layouts, padded(): block = jnp.concatenate([low, block, high], axis=dim)  56.4 us
    dot_general x1, matrix products, local(): lax.dot_general(shard_rows, entries, (((0,), (0,)), ((), ())), preferred_...  55.8 us
    dot_general x1, matrix products, local(): lax.dot_general(entries, surface_load, (((1,), (1,)), ((), ())), preferre...  55.7 us
    ppermute x3, waiting for transfers between devices, local(): lax.ppermute(sums, 'lat', [(dev, dev ^ hop) for dev in range(8)])  51.2 us
  transfers between devices with their start and end apart: 8, of which 5 were waited for; matrix products, arithmetic and copies ran while one was open for 34% of the time, Pallas kernels for 0%

profile of v1, /device:TPU:0, one launch (start us, length us, event | category | flops | bytes accessed | tf_op | source)
XLA Modules:
  0.0 1056.4 jit_solution(10525184374630752660)
XLA Ops:
  94.9 56.4 %concatenate.7 = bf16[7,296,2200]{1,2,0:T(8,128)(2,1)} concatenate(bf16[7,296,20]{1,2,0:T(8,128)(2,1)S(1)} %collective-permute-done.2, bf16[7,296,2160]{1,2,0:T(8,128)(2,1)} %copy-done.7, bf16[7,296,20]{1,2,0:T(8,128)(2,1)S(1)} %collective-permute-done.3), dimensions={2} | concatenate | bytes 18233600 | tf_op jit(solution)/shard_map/concatenate | solution.py:32
  151.3 13.3 %convert_element_type.790 = f32[7,296,2200]{1,2,0:T(8,128)} convert(bf16[7,296,2200]{1,2,0:T(8,128)(2,1)} %concatenate.7) | non-fusion elementwise | flops 4558400 | bytes 27350400 | tf_op jit(solution)/shard_map/convert_element_type | solution.py:164
  171.9 14.8 %slice_bitcast_fusion.1 = (f32[296,2200]{0,1:T(8,128)S(1)}, f32[296,2200]{0,1:T(8,128)}, f32[296,2200]{0,1:T(8,128)}, f32[296,2200]{0,1:T(8,128)}, f32[296,2200]...) fusion(f32[7,296,2200]{1,2,0:T(8,128)} %convert_element_type.790), kind=kLoop, calls=%fused_computation.498 | loop fusion | bytes 36467200 | tf_op jit(solution)/shard_map/squeeze | solution.py:171
  196.4 13.0 %slice_multiply_fusion.11 = (f32[292,2196]{0,1:T(8,128)S(1)}, f32[292,2196]{0,1:T(8,128)}, f32[292,2196]{0,1:T(8,128)}, f32[292,2196]{0,1:T(8,128)}) fusion(f32[296,2200]{0,1:T(8,128)S(1)} %copy-done.3, f32[296,2200]{0,1:T(8,128)S(1)} %get-tuple-element.672, f32[294,2198]{0,1:T(8,128)S(1)} %fusion.173, f32[296,2200]{0,1:T(8,128)} %get-tuple-element.674, ...), kind=kLoop, calls=%fused_computation.711 | loop fusion | flops 18595728 | bytes 35911328 | tf_op jit(solution)/shard_map/mul | solution.py:173
  218.3 19.8 %slice_multiply_fusion.15 = (f32[288,2192]{0,1:T(8,128)}, f32[288,2192]{0,1:T(8,128)}, f32[288,2192]{0,1:T(8,128)}, f32[288,2192]{0,1:T(8,128)}) fusion(f32[296,2200]{0,1:T(8,128)} %get-tuple-element.676, f32[296,2200]{0,1:T(8,128)S(1)} %get-tuple-element.672, f32[290,2194]{0,1:T(8,128)} %fusion.157, f32[292,2196]{0,1:T(8,128)} %get-tuple-element.684, ...), kind=kLoop, calls=%fused_computation.715 | loop fusion | flops 18307584 | bytes 35354880 | tf_op jit(solution)/shard_map/mul | solution.py:173
  249.0 19.2 %slice_multiply_fusion.13 = (f32[284,2188]{0,1:T(8,128)}, f32[284,2188]{0,1:T(8,128)}, f32[284,2188]{0,1:T(8,128)}, f32[284,2188]{0,1:T(8,128)}) fusion(f32[296,2200]{0,1:T(8,128)} %get-tuple-element.676, f32[296,2200]{0,1:T(8,128)S(1)} %get-tuple-element.672, f32[286,2190]{0,1:T(8,128)} %fusion.193, f32[288,2192]{0,1:T(8,128)} %get-tuple-element.682, ...), kind=kLoop, calls=%fused_computation.713 | loop fusion | flops 18020368 | bytes 34800224 | tf_op jit(solution)/shard_map/mul | solution.py:173
  278.2 12.9 %slice_multiply_fusion.19 = (f32[280,2184]{0,1:T(8,128)}, f32[280,2184]{0,1:T(8,128)}, f32[280,2184]{0,1:T(8,128)}, f32[280,2184]{0,1:T(8,128)}) fusion(f32[296,2200]{0,1:T(8,128)S(1)} %copy-done.4, f32[296,2200]{0,1:T(8,128)S(1)} %get-tuple-element.672, f32[282,2186]{0,1:T(8,128)S(1)} %fusion.177, f32[284,2188]{0,1:T(8,128)} %get-tuple-element.688, ...), kind=kLoop, calls=%fused_computation.719 | loop fusion | flops 17734080 | bytes 34247360 | tf_op jit(solution)/shard_map/mul | solution.py:173
  301.1 12.7 %slice_multiply_fusion.17 = (f32[276,2180]{0,1:T(8,128)S(1)}, f32[276,2180]{0,1:T(8,128)}, f32[276,2180]{0,1:T(8,128)}, f32[276,2180]{0,1:T(8,128)}) fusion(f32[296,2200]{0,1:T(8,128)S(1)} %copy-done.4, f32[296,2200]{0,1:T(8,128)S(1)} %get-tuple-element.672, f32[278,2182]{0,1:T(8,128)S(1)} %fusion.225, f32[280,2184]{0,1:T(8,128)} %get-tuple-element.686, ...), kind=kLoop, calls=%fused_computation.717 | loop fusion | flops 17448720 | bytes 33696288 | tf_op jit(solution)/shard_map/mul | solution.py:173
  322.6 19.4 %slice_multiply_fusion.23 = (f32[272,2176]{0,1:T(8,128)}, f32[272,2176]{0,1:T(8,128)}, f32[272,2176]{0,1:T(8,128)}, f32[272,2176]{0,1:T(8,128)}) fusion(f32[296,2200]{0,1:T(8,128)} %get-tuple-element.676, f32[296,2200]{0,1:T(8,128)S(1)} %get-tuple-element.672, f32[274,2178]{0,1:T(8,128)} %fusion.209, f32[276,2180]{0,1:T(8,128)} %get-tuple-element.692, ...), kind=kLoop, calls=%fused_computation.723 | loop fusion | flops 17164288 | bytes 33147008 | tf_op jit(solution)/shard_map/mul | solution.py:173
  353.1 19.2 %slice_multiply_fusion.21 = (f32[268,2172]{0,1:T(8,128)}, f32[268,2172]{0,1:T(8,128)}, f32[268,2172]{0,1:T(8,128)}, f32[268,2172]{0,1:T(8,128)}) fusion(f32[296,2200]{0,1:T(8,128)} %get-tuple-element.676, f32[296,2200]{0,1:T(8,128)S(1)} %get-tuple-element.672, f32[270,2174]{0,1:T(8,128)} %fusion.257, f32[272,2176]{0,1:T(8,128)} %get-tuple-element.690, ...), kind=kLoop, calls=%fused_computation.721 | loop fusion | flops 16880784 | bytes 32599520 | tf_op jit(solution)/shard_map/mul | solution.py:173
  372.3 11.1 %fusion.241 = f32[266,2170]{0,1:T(8,128)} fusion(f32[268,2172]{0,1:T(8,128)} %get-tuple-element.695, f32[268,2172]{0,1:T(8,128)} %get-tuple-element.522, f32[296,2200]{0,1:T(8,128)S(1)} %get-tuple-element.677, f32[270,2174]{0,1:T(8,128)} %fusion.257), kind=kLoop, calls=%fused_computation.616 | loop fusion | flops 4040540 | bytes 16162160 | tf_op jit(solution)/shard_map/sub | solution.py:175
  383.4 18.4 %slice_multiply_fusion.27 = (f32[264,2168]{0,1:T(8,128)}, f32[264,2168]{0,1:T(8,128)}, f32[264,2168]{0,1:T(8,128)}, f32[264,2168]{0,1:T(8,128)}) fusion(f32[296,2200]{0,1:T(8,128)} %get-tuple-element.676, f32[296,2200]{0,1:T(8,128)S(1)} %get-tuple-element.672, f32[266,2170]{0,1:T(8,128)} %fusion.241, f32[268,2172]{0,1:T(8,128)} %get-tuple-element.696, ...), kind=kLoop, calls=%fused_computation.727 | loop fusion | flops 16598208 | bytes 32053824 | tf_op jit(solution)/shard_map/mul | solution.py:173
  401.8 11.1 %fusion.289 = f32[262,2166]{0,1:T(8,128)} fusion(f32[264,2168]{0,1:T(8,128)} %get-tuple-element.693, f32[264,2168]{0,1:T(8,128)} %get-tuple-element.518, f32[296,2200]{0,1:T(8,128)S(1)} %get-tuple-element.677, f32[266,2170]{0,1:T(8,128)} %fusion.241), kind=kLoop, calls=%fused_computation.687 | loop fusion | flops 3972444 | bytes 15889776 | tf_op jit(solution)/shard_map/sub | solution.py:175
  413.0 19.2 %slice_multiply_fusion.25 = (f32[260,2164]{0,1:T(8,128)}, f32[260,2164]{0,1:T(8,128)}, f32[260,2164]{0,1:T(8,128)}, f32[260,2164]{0,1:T(8,128)}) fusion(f32[296,2200]{0,1:T(8,128)} %get-tuple-element.676, f32[296,2200]{0,1:T(8,128)S(1)} %get-tuple-element.672, f32[262,2166]{0,1:T(8,128)} %fusion.289, f32[264,2168]{0,1:T(8,128)} %get-tuple-element.694, ...), kind=kLoop, calls=%fused_computation.725 | loop fusion | flops 16316560 | bytes 31509920 | tf_op jit(solution)/shard_map/mul | solution.py:173
  443.3 15.0 %fusion.307 = (f32[256,2160]{0,1:T(8,128)}, f32[256,2160]{0,1:T(8,128)}, f32[256,2160]{0,1:T(8,128)S(1)}) fusion(f32[296,2200]{0,1:T(8,128)S(1)} %copy-done.2, f32[258,2162]{0,1:T(8,128)} %fusion.273, f32[296,2200]{0,1:T(8,128)} %get-tuple-element.676, f32[260,2164]{0,1:T(8,128)} %get-tuple-element.700, f32[260,2164]{0,1:T(8,128)} %get-tuple-element.515, ...), kind=kLoop, calls=%fused_computation.734 | loop fusion | flops 14929920 | bytes 30967808 | tf_op jit(solution)/shard_map/div | solution.py:201
  459.0 55.7 %fusion.302 = bf16[1440,256]{1,0:T(8,128)(2,1)} fusion(s32[2160]{0:T(1024)S(1)} %copy-done.23, s32[1440]{0:T(1024)S(1)} %copy-done.20, pred[1440]{0:T(1024)(128)(4,1)S(1)} %copy-done.36, bf16[256,2160]{0,1:T(8,128)(2,1)S(1)} %fusion.394), kind=kOutput, calls=%fused_computation.728 | convolution fusion | flops 1633328640 | bytes 1859040 | tf_op jit(solution)/shard_map/dot_general | solution.py:210
  514.8 20.9 %broadcast_in_dim.923.clone = bf16[180,720,256]{2,1,0:T(8,128)(2,1)} broadcast(bf16[]{:T(256)} %constant.625.clone.1), dimensions={} | broadcast | bytes 66355200 | tf_op jit(solution)/shard_map/broadcast_in_dim | solution.py:104
  535.8 331.0 %while.23 = (s32[]{:T(128)}, f32[180,256]{1,0:T(8,128)S(1)}, f32[180,256]{1,0:T(8,128)S(1)}, f32[180,256]{1,0:T(8,128)S(1)}, bf16[180,720,256]{2,1,0:T(8,128)(2,...) while((s32[]{:T(128)}, f32[180,256]{1,0:T(8,128)S(1)}, ...), condition=%wide.region_7.8_spmd.clone, body=%wide.region_6.7_spmd.clone.sunk | while | flops 42912776 | bytes 26192132 | solution.py:125
  868.0 25.3 %convolution_bitcast_fusion = f32[2,180,720]{2,0,1:T(2,128)S(1)} fusion(bf16[180,720,256]{2,1,0:T(8,128)(2,1)} %get-tuple-element.332, f32[2,180,256]{2,1,0:T(8,128)S(1)} %reshape.2027, pred[180,256]{1,0:T(8,128)(4,1)S(1)} %broadcast_compare_fusion, f32[256]{0:T(256)S(1)} %broadcast_multiply_fusion), kind=kOutput, calls=%fused_computation.752 | convolution fusion | flops 132986880 | bytes 67807744 | tf_op jit(solution)/shard_map/knj,pkj->pkn/dot_general | solution.py:234
  899.1 24.7 %collective-permute-done.5 = f32[2,180,720]{2,0,1:T(2,128)S(1)} collective-permute-done((f32[2,180,720]{2,0,1:T(2,128)S(1)}, f32[2,180,720]{2,0,1:T(2,128)S(1)}, u32[]{:S(2)}, u32[]{:S(2)}) %collective-permute-start.5) | collective-permute-done | bytes 1036832 | tf_op jit(solution)/shard_map/ppermute | solution.py:247
  927.6 23.7 %collective-permute-done.6 = f32[2,180,720]{2,0,1:T(2,128)S(1)} collective-permute-done((f32[2,180,720]{2,0,1:T(2,128)S(1)}, f32[2,180,720]{2,0,1:T(2,128)S(1)}, u32[]{:S(2)}, u32[]{:S(2)}) %collective-permute-start.6) | collective-permute-done | bytes 1036832 | tf_op jit(solution)/shard_map/ppermute | solution.py:247
  951.9 23.5 %fusion.318 = bf16[2,180,256]{2,0,1:T(2,128)(2,1)S(1)} fusion(bf16[180,720,256]{2,1,0:T(8,128)(2,1)} %get-tuple-element.332, f32[2,180,720]{2,0,1:T(2,128)S(1)} %add_multiply_fusion), kind=kOutput, calls=%fused_computation.754 | convolution fusion | flops 133061760 | bytes 67576320 | tf_op jit(solution)/shard_map/knj,pkn->pkj/dot_general | solution.py:254
  976.4 17.1 %all_gather.3 = bf16[1440,256]{1,0:T(8,128)(2,1)S(1)} all-gather(bf16[360,256]{1,0:T(8,128)(2,1)S(1)} %reshape.2023), channel_id=1, replica_groups=mesh['lat'=8,'lon'=4] {'lon'}, dimensions={0}, use_global_device_ids=true | all-gather | bytes 921600 | tf_op jit(solution)/shard_map/all_gather | solution.py:258
  993.4 55.8 %fusion.150 = f32[256,2160]{0,1:T(8,128)} fusion(bf16[1440,256]{1,0:T(8,128)(2,1)S(1)} %all_gather.3, f32[1440]{0:T(1024)S(1)} %compare_select_fusion, s32[2160]{0:T(1024)S(1)} %copy-done.23, s32[1440]{0:T(1024)S(1)} %copy-done.20, pred[1440]{0:T(1024)(128)(4,1)S(1)} %copy-done.36), kind=kOutput, calls=%fused_computation.472 | convolution fusion | flops 1632960000 | bytes 2970720 | tf_op jit(solution)/shard_map/dot_general | solution.py:262
  (1511 shorter events, 510.5 us)
Async XLA Ops:
  7.2 859.8 %reduce-scatter.2.cloned.1.call-start = ((), (), s32[]{:S(2)}) async-start(), calls=%async_computation.1 | async-start | bytes 921600 | tf_op jit(solution)/shard_map/reduce_scatter | solution.py:209
  12.5 14.3 %copy-start.10 = (bf16[2,8,256,2160]{2,3,1,0:T(8,128)(2,1)S(1)}, bf16[2,8,256,2160]{2,3,1,0:T(8,128)(2,1)}, u32[]{:S(2)}) copy-start(bf16[2,8,256,2160]{2,3,1,0:T(8,128)(2,1)} %param.18) | copy-start | bytes 53084164
  43.2 12.4 %copy-start.32 = (s32[720]{0:T(1024)S(1)}, s32[720]{0:T(1024)}, u32[]{:S(2)}) copy-start(s32[720]{0:T(1024)} %param.21) | copy-start | bytes 8644
  43.2 20.2 %collective-permute-start.1 = (bf16[7,20,2160]{2,0,1:T(8,128)(2,1)S(1)}, bf16[7,20,2160]{2,0,1:T(8,128)(2,1)S(1)}, u32[]{:S(2)}, u32[]{:S(2)}) collective-permute-start(bf16[7,20,2160]{2,0,1:T(8,128)(2,1)S(1)} %copy.76), channel_id=1, source_target_pairs={{4,0},{8,4},{12,8},{16,12},{20,16},{24,20},{28,24},{5,1},{9,5},{13... | collective-permute-start | bytes 1814408 | tf_op jit(solution)/shard_map/ppermute | solution.py:31
  48.6 11.4 %collective-permute-start = (bf16[7,20,2160]{2,0,1:T(8,128)(2,1)S(1)}, bf16[7,20,2160]{2,0,1:T(8,128)(2,1)S(1)}, u32[]{:S(2)}, u32[]{:S(2)}) collective-permute-start(bf16[7,20,2160]{2,0,1:T(8,128)(2,1)S(1)} %copy.75), channel_id=1, source_target_pairs={{0,4},{4,8},{8,12},{12,16},{16,20},{20,24},{24,28},{1,5},{5,9},{9,... | collective-permute-start | bytes 1814408 | tf_op jit(solution)/shard_map/ppermute | solution.py:28
  81.7 8.9 collective-permute-start.3
  86.8 8.1 collective-permute-start.2
  372.3 11.1 %copy-start.26 = (f32[264]{0:T(512)S(1)}, f32[264]{0:T(512)}, u32[]{:S(2)}) copy-start(f32[264]{0:T(512)} %get-tuple-element.442) | copy-start | bytes 3172
  401.8 11.2 %copy-start.24 = (f32[260]{0:T(512)S(1)}, f32[260]{0:T(512)}, u32[]{:S(2)}) copy-start(f32[260]{0:T(512)} %get-tuple-element.440) | copy-start | bytes 3124
  401.8 11.2 %copy-start.25 = (f32[260]{0:T(512)S(1)}, f32[260]{0:T(512)}, u32[]{:S(2)}) copy-start(f32[260]{0:T(512)} %get-tuple-element.441) | copy-start | bytes 3124
  443.2 15.0 %copy-start.12 = (pred[256,2160]{0,1:T(8,128)(4,1)S(1)}, pred[256,2160]{0,1:T(8,128)(4,1)}, u32[]{:S(2)}) copy-start(pred[256,2160]{0,1:T(8,128)(4,1)} %get-tuple-element.551) | copy-start | bytes 1658884
  458.2 56.5 %copy-start.11 = (f32[256,2160]{0,1:T(8,128)}, f32[256,2160]{0,1:T(8,128)S(1)}, u32[]{:S(2)}) copy-start(f32[256,2160]{0,1:T(8,128)S(1)} %get-tuple-element.705) | copy-start | bytes 6635524
  514.8 21.0 %copy-start.5 = (f32[180,256]{1,0:T(8,128)S(1)}, f32[180,256]{1,0:T(8,128)}, u32[]{:S(2)}) copy-start(f32[180,256]{1,0:T(8,128)} %custom-call.1) | copy-start | bytes 552964
  514.8 20.9 %copy-start.6 = (f32[180,256]{1,0:T(8,128)S(1)}, f32[180,256]{1,0:T(8,128)}, u32[]{:S(2)}) copy-start(f32[180,256]{1,0:T(8,128)} %custom-call) | copy-start | bytes 552964
  514.8 20.9 %copy-start.9 = (f32[180,256]{1,0:T(8,128)S(1)}, f32[180,256]{1,0:T(8,128)}, u32[]{:S(2)}) copy-start(f32[180,256]{1,0:T(8,128)} %multiply_add_fusion) | copy-start | bytes 552964
  514.8 20.9 %copy-start.17 = (f32[180]{0:T(256)S(1)}, f32[180]{0:T(256)}, u32[]{:S(2)}) copy-start(f32[180]{0:T(256)} %get-tuple-element.512) | copy-start | bytes 2164
  514.8 20.9 %copy-start.19 = (f32[180]{0:T(256)S(1)}, f32[180]{0:T(256)}, u32[]{:S(2)}) copy-start(f32[180]{0:T(256)} %copy-done.18) | copy-start | bytes 2164
  535.7 331.1 %copy-start.22 = (s32[180]{0:T(256)S(1)}, s32[180]{0:T(256)}, u32[]{:S(2)}) copy-start(s32[180]{0:T(256)} %copy-done.21) | copy-start | bytes 2164
  535.8 331.1 %copy-start.37 = (s32[256]{0:T(256)S(1)}, s32[256]{0:T(256)}, u32[]{:S(2)}) copy-start(s32[256]{0:T(256)} %param.20) | copy-start | bytes 3076
  893.2 34.2 %copy-start.35 = (s32[720]{0:T(1024)S(1)}, s32[720]{0:T(1024)}, u32[]{:S(2)}) copy-start(s32[720]{0:T(1024)} %param.22) | copy-start | bytes 8644
  893.2 34.2 %copy-start.38 = (f32[64]{0:T(128)S(1)}, f32[64]{0:T(128)}, u32[]{:S(2)}) copy-start(f32[64]{0:T(128)} %param.23) | copy-start | bytes 772
  893.2 2.8 collective-permute-start.4
  896.6 27.1 %collective-permute-start.5 = (f32[2,180,720]{2,0,1:T(2,128)S(1)}, f32[2,180,720]{2,0,1:T(2,128)S(1)}, u32[]{:S(2)}, u32[]{:S(2)}) collective-permute-start(f32[2,180,720]{2,0,1:T(2,128)S(1)} %add.2504), channel_id=1, source_target_pairs={{0,8},{4,12},{8,0},{12,4},{16,24},{20,28},{24,16},{28,20},{1,9},{5... | collective-permute-start | bytes 3110408 | tf_op jit(solution)/shard_map/ppermute | solution.py:247
  924.3 27.0 %collective-permute-start.6 = (f32[2,180,720]{2,0,1:T(2,128)S(1)}, f32[2,180,720]{2,0,1:T(2,128)S(1)}, u32[]{:S(2)}, u32[]{:S(2)}) collective-permute-start(f32[2,180,720]{2,0,1:T(2,128)S(1)} %add.2505), channel_id=1, source_target_pairs={{0,16},{4,20},{8,24},{12,28},{16,0},{20,4},{24,8},{28,12},{1,17},{... | collective-permute-start | bytes 3110408 | tf_op jit(solution)/shard_map/ppermute | solution.py:247
  (23 other events, 158.5 us)
Sparse Core Ops, SparseCore 0:
  514.9 22.8 reduce-scatter.1
